TPU v7x, 128 devices: a whole 4x4x4 slice. The times are simulated.
128 devices in a mesh: dp: 64 (over y, x_hi, z, core), tensor: 2 (over x_lo).
Axes of the slice: x: 4 (x_hi: 2, x_lo: 2; x = x_hi * 2 + x_lo), y: 4, z: 4, core: 2. Of those that a mesh axis runs over, the one named last changes fastest.
Arguments:
- tokens: bfloat16 [32768, 1024], P(('dp', 'tensor')), may hold values from -6 to 6
- gain_attn: float32 [1024], replicated, may hold values from 0.5 to 1.5
- w_query: bfloat16 [1024, 1024], P('dp', 'tensor'), may hold values from -0.25 to 0.25
- w_key: bfloat16 [1024, 1024], P('dp', 'tensor'), may hold values from -0.25 to 0.25
- w_value: bfloat16 [1024, 1024], P('dp', 'tensor'), may hold values from -0.1875 to 0.1875
- w_out: bfloat16 [1024, 1024], P('tensor', 'dp'), may hold values from -1.5 to 1.5
- gain_moe: float32 [1024], replicated, may hold values from 0.5 to 1.5
- w_gate: bfloat16 [32, 1024, 512], P(None, 'dp', 'tensor'), may hold values from -0.1875 to 0.1875
- w_up: bfloat16 [32, 1024, 512], P(None, 'dp', 'tensor'), may hold values from -0.1875 to 0.1875
- w_down: bfloat16 [32, 512, 1024], P(None, 'tensor', 'dp'), may hold values from -1 to 1
- routes: int32 [32768, 8], P('dp'), may hold values from 0 to 31, all different within a row; in each aligned block of 512 rows (0 to 511, 512 to 1023, ...) at most 160 rows name the same one
- route_weights: float32 [32768, 8], P('dp'), may hold values from 0.06 to 0.25
- cotangent: bfloat16 [32768, 1024], P(('dp', 'tensor')), may hold values from -6 to 6
Outputs:
- output: bfloat16 [32768, 1024], P(('dp', 'tensor'))
- grad_tokens: bfloat16 [32768, 1024], P(('dp', 'tensor'))
- grad_gain_attn: float32 [1024], replicated
- grad_query: float32 [1024, 1024], P('dp', 'tensor')
- grad_key: float32 [1024, 1024], P('dp', 'tensor')
- grad_value: float32 [1024, 1024], P('dp', 'tensor')
- grad_out: float32 [1024, 1024], P('tensor', 'dp')
- grad_gain_moe: float32 [1024], replicated
- grad_gate: float32 [32, 1024, 512], P(None, 'dp', 'tensor')
- grad_up: float32 [32, 1024, 512], P(None, 'dp', 'tensor')
- grad_down: float32 [32, 512, 1024], P(None, 'tensor', 'dp')
Inputs may be any that keep to these rules, and one draw needn't show every extreme that they name: `routes`: each token names 8 different experts. Among the 512 tokens of one sequence no expert is named by more than 160 tokens, and in every draw some expert is named by exactly 160.
All inputs are finite; a program needn't handle non-finite values.
Results may differ from a plain program's by a relative error of at most 0.02.
Values may be sent and summed in bfloat16 or wider, within the bound.
No kernel may reach another device: no remote copies, remote signals or barrier semaphores. Data moves between devices by JAX's collectives and lax.ppermute only.
A program may use at most 320 MiB of HBM per device.

v0:
```python
import jax
import jax.numpy as jnp
from jax import lax
from jax.sharding import PartitionSpec as P

HD = 64
CAP = 160


EPSILON = 1e-06
THETA = 10000.0


def rotary_tables(length, head_size):
    half_size = head_size // 2
    frequency = THETA ** (-2.0 * jnp.arange(half_size, dtype=jnp.float32) / head_size)
    angles = jnp.arange(length, dtype=jnp.float32)[:, None] * frequency[None, :]
    return (jnp.cos(angles)[:, None, :], jnp.sin(angles)[:, None, :])


def rotate(heads, cosine_table, sine_table):
    half_size = heads.shape[-1] // 2
    first_half = heads[..., :half_size]
    second_half = heads[..., half_size:]
    return jnp.concatenate(
        [
            first_half * cosine_table - second_half * sine_table,
            second_half * cosine_table + first_half * sine_table,
        ],
        -1,
    )


def unrotate(grads, cosine_table, sine_table):
    half_size = grads.shape[-1] // 2
    first_half = grads[..., :half_size]
    second_half = grads[..., half_size:]
    return jnp.concatenate(
        [
            first_half * cosine_table + second_half * sine_table,
            second_half * cosine_table - first_half * sine_table,
        ],
        -1,
    )


def rms_scale(rows):
    return lax.rsqrt(jnp.mean(rows * rows, -1, keepdims=True) + EPSILON)


def norm_back(rows, scaling, gain, gradient):
    weighted = gradient * gain
    grad_rows = scaling * weighted - rows * (scaling * scaling * scaling) * jnp.mean(
        weighted * rows, -1, keepdims=True
    )
    grad_gain = jnp.sum(gradient * rows * scaling, 0)
    return (grad_rows, grad_gain)


def attend_forward(queries, key_heads, value_heads, scaling):
    length, heads, head_size = queries.shape
    block_rows = min(length, 512)
    blocked = queries.reshape(length // block_rows, block_rows, heads, head_size)

    def one_block(query_rows):
        scores = (
            jnp.einsum("qhd,khd->hqk", query_rows, key_heads, preferred_element_type=jnp.float32)
            * scaling
        )
        row_max = jnp.max(scores, -1, keepdims=True)
        exponent = jnp.exp(scores - row_max)
        totals = jnp.sum(exponent, -1, keepdims=True)
        softmax_w = (exponent / totals).astype(jnp.bfloat16)
        result = jnp.einsum(
            "hqk,khd->qhd", softmax_w, value_heads, preferred_element_type=jnp.float32
        )
        return (result, row_max + jnp.log(totals))

    results, log_sums = lax.map(one_block, blocked)
    return (results.reshape(length, heads * head_size), log_sums)


def attend_backward(queries, key_heads, value_heads, log_sums, grad_mixed, scaling):
    length, heads, head_size = queries.shape
    block_rows = min(length, 512)
    count = length // block_rows
    blocked = queries.reshape(count, block_rows, heads, head_size)
    grad_blocked = grad_mixed.reshape(count, block_rows, heads, head_size)

    def one_block(carried, pieces):
        query_rows, log_rows, grad_rows = pieces
        scores = (
            jnp.einsum("qhd,khd->hqk", query_rows, key_heads, preferred_element_type=jnp.float32)
            * scaling
        )
        softmax_f = jnp.exp(scores - log_rows)
        grad_soft = jnp.einsum(
            "qhd,khd->hqk", grad_rows, value_heads, preferred_element_type=jnp.float32
        )
        grad_scores = (
            softmax_f * (grad_soft - jnp.sum(grad_soft * softmax_f, -1, keepdims=True))
        ).astype(jnp.bfloat16)
        grad_query = (
            jnp.einsum("hqk,khd->qhd", grad_scores, key_heads, preferred_element_type=jnp.float32)
            * scaling
        )
        grad_key = (
            carried[0]
            + jnp.einsum(
                "hqk,qhd->khd", grad_scores, query_rows, preferred_element_type=jnp.float32
            )
            * scaling
        )
        grad_value = carried[1] + jnp.einsum(
            "hqk,qhd->khd",
            softmax_f.astype(jnp.bfloat16),
            grad_rows,
            preferred_element_type=jnp.float32,
        )
        return ((grad_key, grad_value), grad_query)

    initial = (jnp.zeros(key_heads.shape, jnp.float32), jnp.zeros(value_heads.shape, jnp.float32))
    sums_kv, grad_query = lax.scan(one_block, initial, (blocked, log_sums, grad_blocked))
    return (grad_query.reshape(length, heads, head_size), sums_kv[0], sums_kv[1])


def seq_rows(local_rows):
    return lax.all_gather(local_rows, "tensor", axis=0, tiled=True)


def seq_sums(partial_rows):
    return lax.psum_scatter(
        partial_rows.astype(jnp.bfloat16), "tensor", scatter_dimension=0, tiled=True
    ).astype(jnp.float32)


def on_device(
    tokens,
    gain_attn,
    w_query,
    w_key,
    w_value,
    w_out,
    gain_moe,
    w_gate,
    w_up,
    w_down,
    routes,
    route_weights,
    cotangent,
):
    length = routes.shape[0]
    route_count = routes.shape[1]
    experts = w_gate.shape[0]
    head_size = HD
    capacity = CAP
    local_heads = w_query.shape[1] // head_size
    scaling = head_size ** (-0.5)
    cosine_table, sine_table = rotary_tables(length, head_size)

    def gather_attention():
        rows_all = (
            lax.all_gather(w_query, "dp", axis=0, tiled=True),
            lax.all_gather(w_key, "dp", axis=0, tiled=True),
            lax.all_gather(w_value, "dp", axis=0, tiled=True),
        )
        cols_all = lax.all_gather(w_out, "dp", axis=1, tiled=True)
        return (rows_all[0], rows_all[1], rows_all[2], cols_all)

    def gather_experts():
        rows_all = (
            lax.all_gather(w_gate, "dp", axis=1, tiled=True),
            lax.all_gather(w_up, "dp", axis=1, tiled=True),
        )
        cols_all = lax.all_gather(w_down, "dp", axis=2, tiled=True)
        return (rows_all[0], rows_all[1], cols_all)

    query_w, key_w, value_w, out_w = gather_attention()
    resid_in = tokens.astype(jnp.float32)
    scale_attn = rms_scale(resid_in)
    normed = (resid_in * scale_attn * gain_attn).astype(jnp.bfloat16)
    full_norm = seq_rows(normed)
    query_proj = jnp.dot(full_norm, query_w, preferred_element_type=jnp.float32).reshape(
        length, local_heads, head_size
    )
    queries = rotate(query_proj, cosine_table, sine_table).astype(jnp.bfloat16)
    key_proj = jnp.dot(full_norm, key_w, preferred_element_type=jnp.float32).reshape(
        length, local_heads, head_size
    )
    key_heads = rotate(key_proj, cosine_table, sine_table).astype(jnp.bfloat16)
    value_heads = (
        jnp.dot(full_norm, value_w, preferred_element_type=jnp.float32)
        .astype(jnp.bfloat16)
        .reshape(length, local_heads, head_size)
    )
    mixed_f, log_sums = attend_forward(queries, key_heads, value_heads, scaling)
    mixed = mixed_f.astype(jnp.bfloat16)
    hidden = resid_in + seq_sums(jnp.dot(mixed, out_w, preferred_element_type=jnp.float32))
    gate_w, up_w, down_w = gather_experts()
    scale_moe = rms_scale(hidden)
    normed_moe = (hidden * scale_moe * gain_moe).astype(jnp.bfloat16)
    full_moe = seq_rows(normed_moe)
    flat_routes = routes.reshape(-1)
    one_hot = (flat_routes[:, None] == jnp.arange(experts, dtype=jnp.int32)[None, :]).astype(
        jnp.int32
    )
    slot_rank = jnp.sum((jnp.cumsum(one_hot, 0) - 1) * one_hot, 1)
    destination = flat_routes * capacity + slot_rank
    owners = jnp.arange(length * route_count, dtype=jnp.int32) // route_count
    slot_token = jnp.zeros((experts * capacity,), jnp.int32).at[destination].set(owners)
    slot_weight = (
        jnp.zeros((experts * capacity,), jnp.float32).at[destination].set(route_weights.reshape(-1))
    )
    dispatched = full_moe[slot_token].reshape(experts, capacity, -1)
    gate_act = jnp.einsum("ecd,edf->ecf", dispatched, gate_w, preferred_element_type=jnp.float32)
    up_act = jnp.einsum("ecd,edf->ecf", dispatched, up_w, preferred_element_type=jnp.float32)
    activated = jax.nn.silu(gate_act)
    hidden_units = (activated * up_act).astype(jnp.bfloat16)
    expert_out = jnp.einsum(
        "ecf,efd->ecd", hidden_units, down_w, preferred_element_type=jnp.float32
    ).reshape(experts * capacity, -1)
    picked = expert_out[destination].reshape(length, route_count, -1)
    expert_sum = seq_sums(jnp.sum(picked * route_weights[:, :, None], 1))
    output = (hidden + expert_sum).astype(jnp.bfloat16)
    query_w, key_w, value_w, out_w = gather_attention()
    gate_w, up_w, down_w = gather_experts()
    full_grad = seq_rows(cotangent)
    grad_slots = (
        (full_grad[slot_token].astype(jnp.float32) * slot_weight[:, None])
        .astype(jnp.bfloat16)
        .reshape(experts, capacity, -1)
    )
    grad_units = jnp.einsum("ecd,efd->ecf", grad_slots, down_w, preferred_element_type=jnp.float32)
    sigmoid_gate = jax.nn.sigmoid(gate_act)
    grad_gate_act = (
        grad_units * up_act * sigmoid_gate * (1.0 + gate_act * (1.0 - sigmoid_gate))
    ).astype(jnp.bfloat16)
    grad_up_act = (grad_units * activated).astype(jnp.bfloat16)
    down_term = jnp.einsum(
        "ecf,ecd->efd", hidden_units, grad_slots, preferred_element_type=jnp.float32
    )
    gate_term = jnp.einsum(
        "ecd,ecf->edf", dispatched, grad_gate_act, preferred_element_type=jnp.float32
    )
    up_term = jnp.einsum(
        "ecd,ecf->edf", dispatched, grad_up_act, preferred_element_type=jnp.float32
    )
    grad_dispatch = (
        jnp.einsum("ecf,edf->ecd", grad_gate_act, gate_w, preferred_element_type=jnp.float32)
        + jnp.einsum("ecf,edf->ecd", grad_up_act, up_w, preferred_element_type=jnp.float32)
    ).reshape(experts * capacity, -1)
    grad_moe_norm = seq_sums(
        jnp.sum(grad_dispatch[destination].reshape(length, route_count, -1), 1)
    )
    back_moe, gain_moe_term = norm_back(hidden, scale_moe, gain_moe, grad_moe_norm)
    grad_hidden = cotangent.astype(jnp.float32) + back_moe
    grad_expert_rows = (
        lax.psum_scatter(gate_term, "dp", scatter_dimension=1, tiled=True),
        lax.psum_scatter(up_term, "dp", scatter_dimension=1, tiled=True),
    )
    grad_down = lax.psum_scatter(down_term, "dp", scatter_dimension=2, tiled=True)
    full_hidden_grad = seq_rows(grad_hidden.astype(jnp.bfloat16))
    grad_mixed = jnp.einsum(
        "ld,hd->lh", full_hidden_grad, out_w, preferred_element_type=jnp.float32
    ).astype(jnp.bfloat16)
    out_term = jnp.einsum("lh,ld->hd", mixed, full_hidden_grad, preferred_element_type=jnp.float32)
    grad_q, grad_k, grad_v = attend_backward(
        queries,
        key_heads,
        value_heads,
        log_sums,
        grad_mixed.reshape(length, local_heads, head_size),
        scaling,
    )
    grad_q_proj = (
        unrotate(grad_q, cosine_table, sine_table).reshape(length, -1).astype(jnp.bfloat16)
    )
    grad_k_proj = (
        unrotate(grad_k, cosine_table, sine_table).reshape(length, -1).astype(jnp.bfloat16)
    )
    grad_v_proj = grad_v.reshape(length, -1).astype(jnp.bfloat16)
    query_term = jnp.einsum("ld,lh->dh", full_norm, grad_q_proj, preferred_element_type=jnp.float32)
    key_term = jnp.einsum("ld,lh->dh", full_norm, grad_k_proj, preferred_element_type=jnp.float32)
    value_term = jnp.einsum("ld,lh->dh", full_norm, grad_v_proj, preferred_element_type=jnp.float32)
    grad_attn_norm = seq_sums(
        jnp.einsum("lh,dh->ld", grad_q_proj, query_w, preferred_element_type=jnp.float32)
        + jnp.einsum("lh,dh->ld", grad_k_proj, key_w, preferred_element_type=jnp.float32)
        + jnp.einsum("lh,dh->ld", grad_v_proj, value_w, preferred_element_type=jnp.float32)
    )
    back_attn, gain_attn_term = norm_back(resid_in, scale_attn, gain_attn, grad_attn_norm)
    grad_tokens = (grad_hidden + back_attn).astype(jnp.bfloat16)
    grad_attn_rows = (
        lax.psum_scatter(query_term, "dp", scatter_dimension=0, tiled=True),
        lax.psum_scatter(key_term, "dp", scatter_dimension=0, tiled=True),
        lax.psum_scatter(value_term, "dp", scatter_dimension=0, tiled=True),
    )
    grad_out = lax.psum_scatter(out_term, "dp", scatter_dimension=1, tiled=True)
    gain_sums = lax.psum((gain_attn_term, gain_moe_term), ("dp", "tensor"))
    return (
        output,
        grad_tokens,
        gain_sums[0],
        grad_attn_rows[0],
        grad_attn_rows[1],
        grad_attn_rows[2],
        grad_out,
        gain_sums[1],
        grad_expert_rows[0],
        grad_expert_rows[1],
        grad_down,
    )


def solution(mesh):
    placed = (
        P(("dp", "tensor"), None),
        P(),
        P("dp", "tensor"),
        P("dp", "tensor"),
        P("dp", "tensor"),
        P("tensor", "dp"),
        P(),
        P(None, "dp", "tensor"),
        P(None, "dp", "tensor"),
        P(None, "tensor", "dp"),
        P("dp", None),
        P("dp", None),
        P(("dp", "tensor"), None),
    )
    return jax.shard_map(
        on_device,
        mesh=mesh,
        in_specs=placed,
        out_specs=(
            P(("dp", "tensor"), None),
            P(("dp", "tensor"), None),
            P(),
            P("dp", "tensor"),
            P("dp", "tensor"),
            P("dp", "tensor"),
            P("tensor", "dp"),
            P(),
            P(None, "dp", "tensor"),
            P(None, "dp", "tensor"),
            P(None, "tensor", "dp"),
        ),
        check_vma=False,
    )
```

profile of v0, /device:TPU:0, one launch (start us, length us, event | category | flops | bytes accessed | tf_op | source)
XLA Modules:
  0.0 3497.8 jit_solution(7247032392656204793)
XLA Ops:
  14.7 23.4 all-gather.12.cloned.1.call-done
  38.1 70.2 %all-gather.18.cloned.1.call-done = bf16[1024,512]{1,0:T(8,128)(2,1)} async-done(((bf16[16,512]{1,0:T(8,128)(2,1)}), bf16[1024,512]{1,0:T(8,128)(2,1)}) %all-gather.18.cloned.1.call-update) | async-done | bytes 1048592 | tf_op jit(solution)/shard_map/all_gather | solution.py:164
  110.6 63.7 %all-gather.16.cloned.1.call-done = bf16[1024,512]{1,0:T(8,128)(2,1)} async-done(((bf16[16,512]{1,0:T(8,128)(2,1)}), bf16[1024,512]{1,0:T(8,128)(2,1)}) %all-gather.16.cloned.1.call-update) | async-done | bytes 1048592 | tf_op jit(solution)/shard_map/all_gather | solution.py:163
  182.5 57.6 %all-gather.14.cloned.1.call-done = bf16[1024,512]{1,0:T(8,128)(2,1)} async-done(((bf16[16,512]{1,0:T(8,128)(2,1)}), bf16[1024,512]{1,0:T(8,128)(2,1)}) %all-gather.14.cloned.1.call-update) | async-done | bytes 1048592 | tf_op jit(solution)/shard_map/all_gather | solution.py:165
  250.4 55.5 %all-gather.20.cloned.1.call-done = bf16[512,1024]{0,1:T(8,128)(2,1)} async-done(((bf16[512,16]{0,1:T(8,128)(2,1)}), bf16[512,1024]{0,1:T(8,128)(2,1)}) %all-gather.20.cloned.1.call-update) | async-done | bytes 1048592 | tf_op jit(solution)/shard_map/all_gather | solution.py:167
  309.7 18.9 reduce-scatter.12.cloned.1.call-done
  347.1 15.5 scatter_custom_fusion
  362.7 15.5 scatter_custom_fusion.1
  378.4 27.5 gather_fusion.2
  405.9 27.2 gather_fusion
  433.1 70.9 %all-gather.26.cloned.1.call-done = bf16[32,1024,256]{2,1,0:T(8,128)(2,1)} async-done(((bf16[32,16,256]{2,1,0:T(8,128)(2,1)}), bf16[32,1024,256]{2,1,0:T(8,128)(2,1)}) %all-gather.26.cloned.1.call-update) | async-done | bytes 16777232 | tf_op jit(solution)/shard_map/all_gather | solution.py:173
  503.9 14.0 fusion.61
  517.9 104.9 %all-gather.24.cloned.1.call-done = bf16[32,1024,256]{2,1,0:T(8,128)(2,1)} async-done(((bf16[32,16,256]{2,1,0:T(8,128)(2,1)}), bf16[32,1024,256]{2,1,0:T(8,128)(2,1)}) %all-gather.24.cloned.1.call-update) | async-done | bytes 16777232 | tf_op jit(solution)/shard_map/all_gather | solution.py:172
  636.9 105.1 %all-gather.28.cloned.1.call-done = bf16[32,256,1024]{1,2,0:T(8,128)(2,1)} async-done(((bf16[32,256,16]{1,2,0:T(8,128)(2,1)}), bf16[32,256,1024]{1,2,0:T(8,128)(2,1)}) %all-gather.28.cloned.1.call-update) | async-done | bytes 16777232 | tf_op jit(solution)/shard_map/all_gather | solution.py:175
  742.0 17.5 multiply_convert_fusion.1
  759.4 26.5 fusion.63
  786.0 20.4 convolution_add_fusion
  806.3 29.3 gather_fusion.3
  845.1 21.5 reduce-scatter.16.cloned.1.call-done
  871.0 24.9 all-gather.32.cloned.1.call-done
  930.2 29.5 gather_fusion.1
  983.5 16.3 fusion.2
  1001.5 15.8 fusion.71
  1019.1 15.9 fusion.70
  1037.5 67.5 %all-reduce = (f32[1024]{0:T(1024)}, f32[1024]{0:T(1024)}) all-reduce(f32[1024]{0:T(1024)S(1)} %get-tuple-element.49, f32[1024]{0:T(1024)S(1)} %copy-done.50), channel_id=1, replica_groups=mesh['dp'=64,'tensor'=2] {'dp','tensor'}, use_global_device_ids=true, to_apply=%region_19.20 | all-reduce | flops 2048 | bytes 16384 | tf_op jit(solution)/shard_map/psum | solution.py:298
  1107.9 224.4 %reduce-scatter.26.cloned.1.call-done = f32[512,16]{0,1:T(8,128)} async-done(((f32[512,1024]{0,1:T(8,128)}), f32[512,16]{0,1:T(8,128)}) %reduce-scatter.26.cloned.1.call-update) | async-done | bytes 32784 | tf_op jit(solution)/shard_map/reduce_scatter | solution.py:297
  1332.4 332.2 %reduce-scatter.24.cloned.1.call-done = f32[16,512]{1,0:T(8,128)} async-done(((f32[1024,512]{1,0:T(8,128)}), f32[16,512]{1,0:T(8,128)}) %reduce-scatter.24.cloned.1.call-update) | async-done | bytes 32784 | tf_op jit(solution)/shard_map/reduce_scatter | solution.py:295
  1664.6 332.8 %reduce-scatter.20.cloned.1.call-done = f32[16,512]{1,0:T(8,128)} async-done(((f32[1024,512]{1,0:T(8,128)}), f32[16,512]{1,0:T(8,128)}) %reduce-scatter.20.cloned.1.call-update) | async-done | bytes 32784 | tf_op jit(solution)/shard_map/reduce_scatter | solution.py:293
  1997.3 333.1 %reduce-scatter.22.cloned.1.call-done = f32[16,512]{1,0:T(8,128)} async-done(((f32[1024,512]{1,0:T(8,128)}), f32[16,512]{1,0:T(8,128)}) %reduce-scatter.22.cloned.1.call-update) | async-done | bytes 32784 | tf_op jit(solution)/shard_map/reduce_scatter | solution.py:294
  2330.5 385.8 %reduce-scatter.32.cloned.1.call-done = f32[32,256,16]{1,2,0:T(8,128)} async-done(((f32[32,256,1024]{1,2,0:T(8,128)}), f32[32,256,16]{1,2,0:T(8,128)}) %reduce-scatter.32.cloned.1.call-update) | async-done | bytes 524304 | tf_op jit(solution)/shard_map/reduce_scatter | solution.py:261
  2716.3 387.1 %reduce-scatter.30.cloned.1.call-done = f32[32,16,256]{2,1,0:T(8,128)} async-done(((f32[32,1024,256]{2,1,0:T(8,128)}), f32[32,16,256]{2,1,0:T(8,128)}) %reduce-scatter.30.cloned.1.call-update) | async-done | bytes 524304 | tf_op jit(solution)/shard_map/reduce_scatter | solution.py:259
  3103.4 387.2 %reduce-scatter.28.cloned.1.call-done = f32[32,16,256]{2,1,0:T(8,128)} async-done(((f32[32,1024,256]{2,1,0:T(8,128)}), f32[32,16,256]{2,1,0:T(8,128)}) %reduce-scatter.28.cloned.1.call-update) | async-done | bytes 524304 | tf_op jit(solution)/shard_map/reduce_scatter | solution.py:258
  (234 shorter events, 144.4 us)
Async XLA Ops:
  7.2 30.9 all-gather.12.cloned.1.call-start
  11.7 96.6 %all-gather.18.cloned.1.call-start = ((), (), s32[]{:S(2)}) async-start(), calls=%async_computation.14 | async-start | bytes 1064960 | tf_op jit(solution)/shard_map/all_gather | solution.py:164
  12.4 161.8 %all-gather.16.cloned.1.call-start = ((), (), s32[]{:S(2)}) async-start(), calls=%async_computation.13 | async-start | bytes 1064960 | tf_op jit(solution)/shard_map/all_gather | solution.py:163
  13.1 226.9 %all-gather.14.cloned.1.call-start = ((), (), s32[]{:S(2)}) async-start(), calls=%async_computation.12 | async-start | bytes 1064960 | tf_op jit(solution)/shard_map/all_gather | solution.py:165
  13.7 292.2 %all-gather.20.cloned.1.call-start = ((), (), s32[]{:S(2)}) async-start(), calls=%async_computation.15 | async-start | bytes 1064960 | tf_op jit(solution)/shard_map/all_gather | solution.py:167
  14.3 314.3 %reduce-scatter.12.cloned.1.call-start = ((), (), s32[]{:S(2)}) async-start(), calls=%async_computation.16 | async-start | bytes 1572864 | tf_op jit(solution)/shard_map/reduce_scatter | solution.py:132
  14.7 167.8 %copy-start.29 = (f32[512,32]{0,1:T(8,128)}, f32[512,32]{0,1:T(8,128)S(1)}, u32[]{:S(2)}) copy-start(f32[512,32]{0,1:T(8,128)S(1)} %get-tuple-element.83) | copy-start | bytes 196612
  14.7 167.8 %copy-start.31 = (f32[512,32]{0,1:T(8,128)}, f32[512,32]{0,1:T(8,128)S(1)}, u32[]{:S(2)}) copy-start(f32[512,32]{0,1:T(8,128)S(1)} %get-tuple-element.84) | copy-start | bytes 196612
  110.6 129.5 %copy-start.10 = (bf16[512,1024]{1,0:T(8,128)(2,1)S(1)}, bf16[512,1024]{1,0:T(8,128)(2,1)}, u32[]{:S(2)}) copy-start(bf16[512,1024]{1,0:T(8,128)(2,1)} %all-gather.12.cloned.1.call-done) | copy-start | bytes 3145732
  248.3 80.3 %copy-start.1 = (bf16[256,1024]{1,0:T(8,128)(2,1)S(1)}, bf16[256,1024]{1,0:T(8,128)(2,1)}, u32[]{:S(2)}) copy-start(bf16[256,1024]{1,0:T(8,128)(2,1)} %param.13) | copy-start | bytes 1572868
  248.3 82.1 %copy-start.40 = (f32[1024]{0:T(1024)S(1)}, f32[1024]{0:T(1024)}, u32[]{:S(2)}) copy-start(f32[1024]{0:T(1024)} %param.19) | copy-start | bytes 12292
  250.3 85.2 %copy-start.33 = (bf16[8,64,512]{2,1,0:T(8,128)(2,1)}, bf16[8,64,512]{2,1,0:T(8,128)(2,1)S(1)}, u32[]{:S(2)}) copy-start(bf16[8,64,512]{2,1,0:T(8,128)(2,1)S(1)} %fusion.16) | copy-start | bytes 1572868
  250.4 84.3 %copy-start.45 = (s32[512,8]{0,1:T(8,128)S(1)}, s32[512,8]{0,1:T(8,128)}, u32[]{:S(2)}) copy-start(s32[512,8]{0,1:T(8,128)} %param.23) | copy-start | bytes 49156
  250.4 85.0 %copy-start.51 = (f32[512,8]{0,1:T(8,128)S(1)}, f32[512,8]{0,1:T(8,128)}, u32[]{:S(2)}) copy-start(f32[512,8]{0,1:T(8,128)} %param.24) | copy-start | bytes 49156
  308.9 69.5 %all-gather.30.cloned.1.call-start = ((), (), s32[]{:S(2)}) async-start(), calls=%async_computation.22 | async-start | bytes 1572864 | tf_op jit(solution)/shard_map/all_gather | solution.py:128
  309.6 96.3 %all-gather.22.cloned.1.call-start = ((), (), s32[]{:S(2)}) async-start(), calls=%async_computation.17 | async-start | bytes 1572864 | tf_op jit(solution)/shard_map/all_gather | solution.py:128
  332.5 171.4 %all-gather.26.cloned.1.call-start = ((), (), s32[]{:S(2)}) async-start(), calls=%async_computation.19 | async-start | bytes 17039360 | tf_op jit(solution)/shard_map/all_gather | solution.py:173
  333.3 289.6 %all-gather.24.cloned.1.call-start = ((), (), s32[]{:S(2)}) async-start(), calls=%async_computation.18 | async-start | bytes 17039360 | tf_op jit(solution)/shard_map/all_gather | solution.py:172
  333.9 408.1 %all-gather.28.cloned.1.call-start = ((), (), s32[]{:S(2)}) async-start(), calls=%async_computation.20 | async-start | bytes 17039360 | tf_op jit(solution)/shard_map/all_gather | solution.py:175
  334.6 531.9 %reduce-scatter.16.cloned.1.call-start = ((), (), s32[]{:S(2)}) async-start(), calls=%async_computation.23 | async-start | bytes 1572864 | tf_op jit(solution)/shard_map/reduce_scatter | solution.py:132
  378.3 363.7 %copy-start.36 = (f32[32,160]{1,0:T(8,128)}, f32[32,160]{1,0:T(8,128)S(1)}, u32[]{:S(2)}) copy-start(f32[32,160]{1,0:T(8,128)S(1)} %mul.511) | copy-start | bytes 61444
  845.0 50.9 %all-gather.32.cloned.1.call-start = ((), (), s32[]{:S(2)}) async-start(), calls=%async_computation.24 | async-start | bytes 1572864 | tf_op jit(solution)/shard_map/all_gather | solution.py:128
  870.9 164.2 %reduce-scatter.18.cloned.1.call-start = ((), (), s32[]{:S(2)}) async-start(), calls=%async_computation.25 | async-start | bytes 1572864 | tf_op jit(solution)/shard_map/reduce_scatter | solution.py:132
  916.7 188.3 %reduce-scatter.14.cloned.1.call-start = ((), (), s32[]{:S(2)}) async-start(), calls=%async_computation.21 | async-start | bytes 1572864 | tf_op jit(solution)/shard_map/reduce_scatter | solution.py:132
  969.2 363.1 %reduce-scatter.26.cloned.1.call-start = ((), (), s32[]{:S(2)}) async-start(), calls=%async_computation.29 | async-start | bytes 2129920 | tf_op jit(solution)/shard_map/reduce_scatter | solution.py:297
  972.8 691.8 %reduce-scatter.24.cloned.1.call-start = ((), (), s32[]{:S(2)}) async-start(), calls=%async_computation.28 | async-start | bytes 2129920 | tf_op jit(solution)/shard_map/reduce_scatter | solution.py:295
  976.3 1021.0 %reduce-scatter.20.cloned.1.call-start = ((), (), s32[]{:S(2)}) async-start(), calls=%async_computation.26 | async-start | bytes 2129920 | tf_op jit(solution)/shard_map/reduce_scatter | solution.py:293
  980.0 1350.5 %reduce-scatter.22.cloned.1.call-start = ((), (), s32[]{:S(2)}) async-start(), calls=%async_computation.27 | async-start | bytes 2129920 | tf_op jit(solution)/shard_map/reduce_scatter | solution.py:294
  983.4 1732.9 %reduce-scatter.32.cloned.1.call-start = ((), (), s32[]{:S(2)}) async-start(), calls=%async_computation.32 | async-start | bytes 34078720 | tf_op jit(solution)/shard_map/reduce_scatter | solution.py:261
  999.8 2103.6 %reduce-scatter.30.cloned.1.call-start = ((), (), s32[]{:S(2)}) async-start(), calls=%async_computation.31 | async-start | bytes 34078720 | tf_op jit(solution)/shard_map/reduce_scatter | solution.py:259
  1017.4 2473.2 %reduce-scatter.28.cloned.1.call-start = ((), (), s32[]{:S(2)}) async-start(), calls=%async_computation.30 | async-start | bytes 34078720 | tf_op jit(solution)/shard_map/reduce_scatter | solution.py:258
  1035.0 70.0 %copy-start.9 = (bf16[256,1024]{1,0:T(8,128)(2,1)S(1)}, bf16[256,1024]{1,0:T(8,128)(2,1)}, u32[]{:S(2)}) copy-start(bf16[256,1024]{1,0:T(8,128)(2,1)} %reduce-scatter.12.cloned.1.call-done) | copy-start | bytes 1572868
  (52 other events, 1106.7 us)
Sparse Core Ops, SparseCore 0:
  11.8 26.2 all-gather.11
  41.4 66.8 all-gather.17
  111.6 62.6 all-gather.15
  177.4 62.6 all-gather.13
  243.2 62.6 all-gather.19
  309.0 19.5 reduce-scatter.11
  330.4 24.7 all-gather.29
  357.5 24.8 all-gather.21
  385.7 118.1 all-gather.25
  507.1 115.7 all-gather.23
  626.2 115.7 all-gather.27
  845.1 21.3 reduce-scatter.15
  871.0 24.7 all-gather.31
  916.8 23.7 reduce-scatter.17
  969.4 23.8 reduce-scatter.13
  996.1 336.2 reduce-scatter.25
  1335.3 329.2 reduce-scatter.23
  1667.3 329.9 reduce-scatter.19
  2000.4 330.0 reduce-scatter.21
  2333.3 382.9 reduce-scatter.31
  2719.2 384.0 reduce-scatter.29
  3106.4 384.1 reduce-scatter.27
where the time goes:
time: 3510 us; the launch traced here: 3500 us
  waiting for transfers between devices  3000 us (85%)
  matrix products  201 us (6%)
  local copies, waits for them, and re-layouts  154 us (4%)
  blocking collectives  67.5 us (2%)
  other arithmetic  54.2 us (2%)
    reduce_scatter x1, waiting for transfers between devices, on_device(): lax.psum_scatter(gate_term, 'dp', scatter_dimension=1, tiled=True)  387 us
    reduce_scatter x1, waiting for transfers between devices, on_device(): lax.psum_scatter(up_term, 'dp', scatter_dimension=1, tiled=True)  387 us
    reduce_scatter x1, waiting for transfers between devices, on_device(): lax.psum_scatter(down_term, 'dp', scatter_dimension=2, tiled=True)  386 us
    reduce_scatter x1, waiting for transfers between devices, on_device(): lax.psum_scatter(key_term, 'dp', scatter_dimension=0, tiled=True)  333 us
    reduce_scatter x1, waiting for transfers between devices, on_device(): lax.psum_scatter(query_term, 'dp', scatter_dimension=0, tiled=True)  333 us
    reduce_scatter x1, waiting for transfers between devices, on_device(): lax.psum_scatter(value_term, 'dp', scatter_dimension=0, tiled=True)  332 us
    reduce_scatter x1, waiting for transfers between devices, on_device(): grad_out = lax.psum_scatter(out_term, 'dp', scatter_dimension=1, tiled=True)  224 us
    all_gather x1, waiting for transfers between devices, gather_experts(): cols_all = lax.all_gather(w_down, 'dp', axis=2, tiled=True)  105 us
  transfers between devices with their start and end apart: 22, of which 18 were waited for; matrix products, arithmetic and copies ran while one was open for 8% of the time, Pallas kernels for 0%

commit v1 on v0

v1 whole, which is shorter than its diff:
```python
import jax
import jax.numpy as jnp
from jax import lax
from jax.experimental import pallas as pl
from jax.experimental.pallas import tpu as pltpu
from jax.sharding import Mesh
from jax.sharding import PartitionSpec as P

HD = 64
CAP = 160
EPSILON = 1e-06
THETA = 10000.0
LOCAL_E = 4
F32 = jnp.float32
BF16 = jnp.bfloat16
VMEM_BYTES = 60 * 1024 * 1024


def swap_x(value, bits):
    return lax.ppermute(value, ("xh", "xl"), [(i, i ^ bits) for i in range(4)])


def swap_c(value):
    return lax.ppermute(value, "c", [(0, 1), (1, 0)])


def swap_4(value, axis, bits):
    return lax.ppermute(value, axis, [(i, i ^ bits) for i in range(4)])


def flip(value, axis, bit):
    return jnp.where(bit == 1, jnp.flip(value, axis), value)


def gather_group(value, order=(2, 3, 1)):
    pieces = {(0, 0): value, (1, 0): swap_c(value)}
    for x in order:
        pieces[0, x] = swap_x(value, x)
        pieces[1, x] = swap_c(pieces[0, x])
    return pieces


def exchange_group(near, far):
    other = swap_c(far)
    both = [jnp.stack([near[x], other[x]]) for x in range(4)]
    return [both[0]] + [swap_x(both[x], x) for x in (1, 2, 3)]


def scatter_group(near, far):
    other = swap_c(far)
    sums = [(near[x].astype(F32) + other[x].astype(F32)).astype(BF16) for x in range(4)]
    return [sums[0]] + [swap_x(sums[x], x) for x in (2, 3, 1)]


def dot(a, b, ca, cb):
    return lax.dot_general(a, b, (((ca,), (cb,)), ((), ())), preferred_element_type=F32)


def whole(n):
    return [pl.BlockSpec(memory_space=pltpu.VMEM)] * n


def kernel_call(body, ins, outs, name, scratch=(), smem=0):
    specs = [pl.BlockSpec(memory_space=pltpu.SMEM)] * smem + whole(len(ins) - smem)
    return pl.pallas_call(
        body,
        out_shape=outs,
        in_specs=specs,
        out_specs=whole(len(outs)),
        scratch_shapes=list(scratch),
        compiler_params=pltpu.CompilerParams(vmem_limit_bytes=VMEM_BYTES),
        name=name,
    )(*ins)


def shape(*dims, dtype=BF16):
    return jax.ShapeDtypeStruct(dims, dtype)


def assemble_body(ids, p0, p1, p2, p3, qkv_ref, out_ref):
    for y, piece in enumerate((p0, p1, p2, p3)):
        for z in range(4):
            for xh in range(2):
                row = ((y ^ ids[0]) * 8 + xh * 4 + (z ^ ids[1])) * 32
                rows = pl.ds(pl.multiple_of(row, 32), 32)
                part = piece[z, xh * 32 : xh * 32 + 32, :]
                qkv_ref[rows, :] = part[:, :384]
                out_ref[rows, :] = part[:, 384:]


def rotated(v, cos, sin):
    lane = lax.broadcasted_iota(jnp.int32, v.shape, 1)
    other = jnp.where(lane % HD < HD // 2, pltpu.roll(v, 96, 1), pltpu.roll(v, 32, 1))
    return v * cos + other * sin


def attend_body(*refs):
    token_refs = refs[:8]
    gain, w_qkv, cos_ref, sin_ref = refs[8:12]
    n1_ref, qkv_ref, near_ref, far_ref = refs[12:]
    cos, sin = cos_ref[...], sin_ref[...]
    for s in range(4):
        for half in range(2):
            x = token_refs[2 * s + half][...].astype(F32)
            r1 = lax.rsqrt(jnp.mean(x * x, -1, keepdims=True) + EPSILON)
            n1_ref[s, half * 256 : half * 256 + 256, :] = (x * r1 * gain[...]).astype(BF16)
        proj = jnp.dot(n1_ref[s], w_qkv[...], preferred_element_type=F32)
        q = rotated(proj[:, :128], cos, sin).astype(BF16)
        k = rotated(proj[:, 128:256], cos, sin).astype(BF16)
        v = proj[:, 256:].astype(BF16)
        qkv_ref[s, :, :128] = q
        qkv_ref[s, :, 128:256] = k
        qkv_ref[s, :, 256:] = v
        mixed = []
        for h in range(2):
            cols = slice(h * HD, h * HD + HD)
            scores = dot(q[:, cols], k[:, cols], 1, 1) * (HD**-0.5)
            e = jnp.exp(scores - jnp.max(scores, -1, keepdims=True))
            p = (e / jnp.sum(e, -1, keepdims=True)).astype(BF16)
            mixed.append(dot(p, v[:, cols], 1, 0).astype(BF16))
        out = jnp.concatenate(mixed, 1)
        dst = near_ref if s < 2 else far_ref
        dst[2 * (s % 2)] = out[:256]
        dst[2 * (s % 2) + 1] = out[256:]


def project_body(*refs):
    tokens, gain = refs[:2]
    mixed = refs[2:6]
    weights = refs[6:14]
    hidden_ref, n2_ref, mixed_ref, wo_ref = refs[14:]
    for c in range(2):
        for x in range(4):
            k = c * 4 + x
            mixed_ref[:, k * 128 : k * 128 + 128] = mixed[x][c]
            wo_ref[:, k * 128 : k * 128 + 128] = weights[k][...]
    hidden = tokens[...].astype(F32) + dot(mixed_ref[...], wo_ref[...], 1, 1)
    hidden_ref[...] = hidden
    r2 = lax.rsqrt(jnp.mean(hidden * hidden, -1, keepdims=True) + EPSILON)
    n2_ref[...] = (hidden * r2 * gain[...]).astype(BF16)


def expert_pieces():
    for y in range(4):
        for z in range(4):
            for c in range(2):
                for xh in range(2):
                    for xl in range(2):
                        row = y * 256 + xh * 128 + z * 32 + c * 16
                        yield y * 4 + z, c * 4 + xh * 2 + xl, slice(row, row + 16), slice(
                            xl * 256, xl * 256 + 256
                        )


def expert_body(*refs):
    n2 = refs[:8]
    ct = refs[8:16]
    rank_ref, share_ref, w_ref = refs[16:19]
    z_near, z_far, g_near, g_far, dw_ref = refs[19:24]
    wg, wu, wd, x_s, gz_s, p_s, z_s, gx_s = refs[24:]
    e = pl.program_id(0)
    rows = 4 * CAP
    for piece, source, d, f in expert_pieces():
        wg[d, f] = w_ref[piece, source, 0, 0]
        wu[d, f] = w_ref[piece, source, 1, 0]
        wd[d, f] = w_ref[piece, source, 2, 0]
    shares = []
    slot = lax.broadcasted_iota(jnp.int32, (CAP, 512), 0)
    for s in range(4):
        hit = slot == rank_ref[0, s : s + 1, :]
        share = jnp.sum(jnp.where(hit, share_ref[0, s : s + 1, :], 0.0), 1, keepdims=True)
        shares.append(share)
        p = hit.astype(F32).astype(BF16)
        p_s[s, pl.ds(pl.multiple_of(e * CAP, 32), CAP), :] = p
        here = slice(s * CAP, s * CAP + CAP)
        x_s[here, :] = (
            dot(p[:, :256], n2[2 * s][...], 1, 0) + dot(p[:, 256:], n2[2 * s + 1][...], 1, 0)
        ).astype(BF16)
        gz_s[here, :] = (
            (dot(p[:, :256], ct[2 * s][...], 1, 0) + dot(p[:, 256:], ct[2 * s + 1][...], 1, 0))
            * share
        ).astype(BF16)
    share = jnp.concatenate(shares, 0)
    a = dot(x_s[...], wg[...], 1, 0)
    b = dot(x_s[...], wu[...], 1, 0)
    sig = 1.0 / (1.0 + jnp.exp(-a))
    sa = a * sig
    u = (sa * b).astype(BF16)
    gu = dot(gz_s[...], wd[...], 1, 0)
    ga = (gu * b * sig * (1.0 + a * (1.0 - sig))).astype(BF16)
    gb = (gu * sa).astype(BF16)
    z = (dot(u, wd[...], 1, 1) * share).astype(BF16)
    gx = (dot(ga, wg[...], 1, 1) + dot(gb, wu[...], 1, 1)).astype(BF16)
    for s in range(4):
        here = slice(s * CAP, s * CAP + CAP)
        there = pl.ds(pl.multiple_of(e * CAP, 32), CAP)
        z_s[s, there, :] = z[here]
        gx_s[s, there, :] = gx[here]
    for m, term in enumerate((dot(x_s[...], ga, 0, 0), dot(x_s[...], gb, 0, 0), dot(gz_s[...], u, 0, 0))):
        term = term.astype(BF16)
        for piece, source, d, f in expert_pieces():
            dw_ref[piece, source, m, 0] = term[d, f]

    @pl.when(e == LOCAL_E - 1)
    def _():
        for s in range(4):
            for src, near, far in ((z_s, z_near, z_far), (gx_s, g_near, g_far)):
                total = dot(p_s[s], src[s], 0, 0).astype(BF16)
                dst = near if s < 2 else far
                dst[2 * (s % 2)] = total[:256]
                dst[2 * (s % 2) + 1] = total[256:]


def run_experts(n2, ct, rank, share, weights):
    block = (16, 8, 3, 1, 16, 256)
    w_spec = pl.BlockSpec(block, lambda e: (0, 0, 0, e, 0, 0))
    table = pl.BlockSpec((1, 4, 512), lambda e: (e, 0, 0))
    blocks = shape(4, 256, 1024)
    return pl.pallas_call(
        expert_body,
        grid=(LOCAL_E,),
        out_shape=(blocks,) * 4 + (shape(16, 8, 3, LOCAL_E, 16, 256),),
        in_specs=whole(16) + [table, table, w_spec],
        out_specs=whole(4) + [w_spec],
        scratch_shapes=[
            pltpu.VMEM((1024, 512), BF16),
            pltpu.VMEM((1024, 512), BF16),
            pltpu.VMEM((1024, 512), BF16),
            pltpu.VMEM((4 * CAP, 1024), BF16),
            pltpu.VMEM((4 * CAP, 1024), BF16),
            pltpu.VMEM((4, LOCAL_E * CAP, 512), BF16),
            pltpu.VMEM((4, LOCAL_E * CAP, 1024), BF16),
            pltpu.VMEM((4, LOCAL_E * CAP, 1024), BF16),
        ],
        compiler_params=pltpu.CompilerParams(vmem_limit_bytes=VMEM_BYTES),
        name="experts",
    )(*n2, *ct, rank, share, weights)


def hidden_back_body(g0, g1, g2, g3, hidden_ref, ct, gain, wo, gh_ref, ghb_ref, near_ref, far_ref, dgain_ref):
    gn2 = g0[...].astype(F32) + g1[...].astype(F32) + g2[...].astype(F32) + g3[...].astype(F32)
    hidden = hidden_ref[...]
    r2 = lax.rsqrt(jnp.mean(hidden * hidden, -1, keepdims=True) + EPSILON)
    w2 = gn2 * gain[...]
    gh = ct[...].astype(F32) + r2 * w2 - hidden * (r2 * r2 * r2) * jnp.mean(w2 * hidden, -1, keepdims=True)
    gh_ref[...] = gh
    ghb = gh.astype(BF16)
    ghb_ref[...] = ghb
    gm = dot(ghb, wo[...], 1, 0).astype(BF16)
    for x in range(4):
        near_ref[x] = gm[:, x * 128 : x * 128 + 128]
        far_ref[x] = gm[:, 512 + x * 128 : 512 + x * 128 + 128]
    dgain_ref[...] = jnp.sum(gn2 * hidden * r2, 0, keepdims=True)


def out_grad_body(ghb, mixed, near_ref, far_ref):
    term = dot(ghb[...], mixed[...], 0, 0).astype(BF16)
    for x in range(4):
        near_ref[x] = term[:, x * 128 : x * 128 + 128]
        far_ref[x] = term[:, 512 + x * 128 : 512 + x * 128 + 128]


def attend_back_body(qkv, m0, m1, m2, m3, cos_ref, sin_ref, near_ref, far_ref):
    gm_refs = (m0, m1, m2, m3)
    cos, sin = cos_ref[...], -sin_ref[...]
    for s in range(4):
        c, x = s // 2, 2 * (s % 2)
        gm = jnp.concatenate([gm_refs[x][c], gm_refs[x + 1][c]], 0)
        gqs, gks, gvs = [], [], []
        for h in range(2):
            q = qkv[s, :, h * HD : h * HD + HD]
            k = qkv[s, :, 128 + h * HD : 128 + h * HD + HD]
            v = qkv[s, :, 256 + h * HD : 256 + h * HD + HD]
            gmh = gm[:, h * HD : h * HD + HD]
            scores = dot(q, k, 1, 1) * (HD**-0.5)
            e = jnp.exp(scores - jnp.max(scores, -1, keepdims=True))
            p = e / jnp.sum(e, -1, keepdims=True)
            gp = dot(gmh, v, 1, 1)
            gs = (p * (gp - jnp.sum(gp * p, -1, keepdims=True))).astype(BF16)
            gqs.append(dot(gs, k, 1, 0) * (HD**-0.5))
            gks.append(dot(gs, q, 0, 0) * (HD**-0.5))
            gvs.append(dot(p.astype(BF16), gmh, 0, 0))
        gq = rotated(jnp.concatenate(gqs, 1), cos, sin).astype(BF16)
        gk = rotated(jnp.concatenate(gks, 1), cos, sin).astype(BF16)
        gv = jnp.concatenate(gvs, 1).astype(BF16)
        dst = near_ref if s < 2 else far_ref
        for j, g in enumerate((gq, gk, gv)):
            dst[x, :, j * 128 : j * 128 + 128] = g[:256]
            dst[x + 1, :, j * 128 : j * 128 + 128] = g[256:]


def attend_grad_body(ids, n1, near, far, w_qkv, gain, pieces_ref, dgain_ref, total):
    for s in range(4):
        src = near if s < 2 else far
        x = 2 * (s % 2)
        term = dot(n1[s, :256], src[x], 0, 0) + dot(n1[s, 256:], src[x + 1], 0, 0)
        total[...] = term if s == 0 else total[...] + term
    weighted = total[...] * w_qkv[...].astype(F32)
    ones = jnp.ones((8, 384), F32)
    sums = lax.dot_general(
        ones,
        weighted,
        (((1,), (1,)), ((), ())),
        precision=lax.Precision.HIGHEST,
        preferred_element_type=F32,
    )
    dgain_ref[...] = sums[:1] / gain[...]
    for y in range(4):
        for z in range(4):
            for xh in range(2):
                row = ((y ^ ids[0]) * 8 + xh * 4 + (z ^ ids[1])) * 32
                part = total[pl.ds(pl.multiple_of(row, 32), 32), :]
                pieces_ref[y, z, xh * 32 : xh * 32 + 32, :] = part.astype(BF16)


def arrange_body(ids, w0, w1, w2, w3, pieces_ref, total):
    total[...] = sum(w[...].astype(F32) for w in (w0, w1, w2, w3))
    for y in range(4):
        for z in range(4):
            for xh in range(2):
                row = ((y ^ ids[0]) * 8 + xh * 4 + (z ^ ids[1])) * 32
                part = total[pl.ds(pl.multiple_of(row, 32), 32), :]
                pieces_ref[y, z, xh * 32 : xh * 32 + 32, :] = part.astype(BF16)


def tokens_back_body(*refs):
    g = refs[:4]
    weights = refs[4:12]
    tokens, gain, gh, out_ref = refs[12:]
    gn1 = jnp.zeros((256, 1024), F32)
    for c in range(2):
        for x in range(4):
            gn1 = gn1 + dot(g[x][c], weights[c * 4 + x][...], 1, 1)
    x = tokens[...].astype(F32)
    r1 = lax.rsqrt(jnp.mean(x * x, -1, keepdims=True) + EPSILON)
    w1 = gn1 * gain[...]
    out_ref[...] = (
        gh[...] + r1 * w1 - x * (r1 * r1 * r1) * jnp.mean(w1 * x, -1, keepdims=True)
    ).astype(BF16)


def pieces_in_order(pieces):
    return [pieces[c, x] for c in range(2) for x in range(4)]


def route_tables(routes, route_weights, c, xh, xl):
    table = jnp.concatenate([routes.T.astype(F32), route_weights.T], 0)
    other = swap_c(table)
    tables = jnp.stack([table, swap_x(table, 2), other, swap_x(other, 2)])
    tables = flip(tables.reshape(4, 16, 2, 256), 2, xl).reshape(4, 16, 512)
    first = ((c * 4 + xh * 2 + xl) * LOCAL_E).astype(F32)
    names = first + jnp.arange(LOCAL_E, dtype=F32)
    match = tables[None, :, :8, :] == names[:, None, None, None]
    share = jnp.sum(jnp.where(match, tables[None, :, 8:, :], 0.0), 2)
    named = jnp.any(match, 2)
    before = (jnp.arange(512)[:, None] <= jnp.arange(512)[None, :]).astype(BF16)
    count = jnp.dot(named.astype(BF16), before, preferred_element_type=F32)
    rank = jnp.where(named, count.astype(jnp.int32) - 1, -1)
    return rank, share


def all_sum(value):
    value = value.reshape(8, 128)
    value = value + swap_c(value)
    value = value + (swap_x(value, 1) + swap_x(value, 2) + swap_x(value, 3))
    for axis in ("y", "z"):
        value = value + (swap_4(value, axis, 1) + swap_4(value, axis, 2) + swap_4(value, axis, 3))
    return value.reshape(1024)


def on_device(
    tokens,
    gain_attn,
    w_query,
    w_key,
    w_value,
    w_out,
    gain_moe,
    w_gate,
    w_up,
    w_down,
    routes,
    route_weights,
    cotangent,
):
    y, xh, z, c, xl = (lax.axis_index(a) for a in ("y", "xh", "z", "c", "xl"))
    ids = jnp.stack([y, z]).astype(jnp.int32)
    gain_attn = gain_attn.reshape(1, 1024)
    gain_moe = gain_moe.reshape(1, 1024)

    mine = jnp.stack([w_query, w_key, w_value, w_out.T], 1)
    mine = mine.reshape(16, 4, 2, 2, 128).transpose(2, 3, 0, 1, 4)
    mine = flip(flip(mine, 0, xh), 1, c).reshape(2, 2, 16, 512)
    got = jnp.stack([mine[0, 0], swap_c(mine[0, 1]), swap_x(mine[1, 0], 2), swap_x(swap_c(mine[1, 1]), 2)])
    got = flip(flip(got.reshape(2, 2, 16, 512), 0, xh), 1, c).reshape(64, 512)
    zs = jnp.stack([got] + [swap_4(got, "z", k) for k in (1, 2, 3)])
    ys = [zs] + [swap_4(zs, "y", k) for k in (1, 2, 3)]
    w_qkv, w_o = kernel_call(
        assemble_body, [ids, *ys], (shape(1024, 384), shape(1024, 128)), "assemble", smem=1
    )

    blocks = gather_group(tokens)

    local = jnp.stack([w_gate, w_up, jnp.swapaxes(w_down, 1, 2)])
    local = local.reshape(3, 8, LOCAL_E, 16, 256).swapaxes(0, 1)
    owned = lax.all_to_all(local, ("c", "xh", "xl"), 0, 0, tiled=True)
    experts = lax.all_gather(owned, ("y", "z"), axis=0)

    rank, share = route_tables(routes, route_weights, c, xh, xl)

    half = HD // 2
    frequency = THETA ** (-2.0 * jnp.arange(half, dtype=F32) / HD)
    place = jnp.arange(512)
    place = ((place // 256) ^ xl) * 256 + place % 256
    angles = place.astype(F32)[:, None] * frequency[None, :]
    cos, sin = jnp.cos(angles), jnp.sin(angles)
    cos = jnp.concatenate([cos] * 4, 1)
    sin = jnp.concatenate([-sin, sin, -sin, sin], 1)

    n1, qkv, near, far = kernel_call(
        attend_body,
        [*pieces_in_order(blocks), gain_attn, w_qkv, cos, sin],
        (shape(4, 512, 1024), shape(4, 512, 384), shape(4, 256, 128), shape(4, 256, 128)),
        "attend",
    )
    w_o_all = pieces_in_order(gather_group(w_o))
    mixed = exchange_group(near, far)
    hidden, n2, mixed, w_o_full = kernel_call(
        project_body,
        [tokens, gain_moe, *mixed, *w_o_all],
        (shape(256, 1024, dtype=F32), shape(256, 1024), shape(256, 1024), shape(1024, 1024)),
        "project",
    )
    n2_all = gather_group(n2)
    cot_all = gather_group(cotangent)
    z_near, z_far, g_near, g_far, grads = run_experts(
        pieces_in_order(n2_all), pieces_in_order(cot_all), rank, share, experts
    )
    reduced = lax.psum_scatter(grads, ("y", "z"), scatter_dimension=0)
    gn2 = scatter_group(g_near, g_far)
    gh, ghb, near, far, dgain_moe = kernel_call(
        hidden_back_body,
        [*gn2, hidden, cotangent, gain_moe, w_o_full],
        (
            shape(256, 1024, dtype=F32),
            shape(256, 1024),
            shape(4, 256, 128),
            shape(4, 256, 128),
            shape(1, 1024, dtype=F32),
        ),
        "hidden_back",
    )
    gm = exchange_group(near, far)
    near, far = kernel_call(
        attend_back_body,
        [qkv, *gm, cos, sin],
        (shape(4, 256, 384), shape(4, 256, 384)),
        "attend_back",
    )
    w_qkv_all = pieces_in_order(gather_group(w_qkv))
    g = exchange_group(near, far)
    grad_tokens = kernel_call(
        tokens_back_body,
        [*g, *w_qkv_all, tokens, gain_attn, gh],
        (shape(256, 1024),),
        "tokens_back",
    )[0]
    qkv_pieces, dgain_attn = kernel_call(
        attend_grad_body,
        [ids, n1, near, far, w_qkv, gain_attn],
        (shape(4, 4, 64, 384), shape(1, 1024, dtype=F32)),
        "attend_grad",
        scratch=[pltpu.VMEM((1024, 384), F32)],
        smem=1,
    )
    near, far = kernel_call(
        out_grad_body, [ghb, mixed], (shape(4, 1024, 128), shape(4, 1024, 128)), "out_grad"
    )
    out_pieces = kernel_call(
        arrange_body,
        [ids, *scatter_group(near, far)],
        (shape(4, 4, 64, 128),),
        "arrange",
        scratch=[pltpu.VMEM((1024, 128), F32)],
        smem=1,
    )[0]
    pieces = jnp.concatenate([qkv_pieces, out_pieces], 3)
    sums = sum([pieces[0].astype(F32)] + [swap_4(pieces[k], "y", k).astype(F32) for k in (1, 2, 3)])
    sums = sums.astype(BF16)
    sums = sum([sums[0].astype(F32)] + [swap_4(sums[k], "z", k).astype(F32) for k in (1, 2, 3)])
    back = flip(flip(sums.reshape(2, 2, 16, 512), 0, xh), 1, c)
    got = jnp.stack([back[0, 0], swap_c(back[0, 1]), swap_x(back[1, 0], 2), swap_x(swap_c(back[1, 1]), 2)])
    got = flip(flip(got.reshape(2, 2, 16, 4, 128), 0, xh), 1, c)
    got = got.transpose(3, 2, 0, 1, 4).reshape(4, 16, 512)

    back = lax.all_to_all(reduced, ("c", "xh", "xl"), 0, 0, tiled=True)
    back = back.swapaxes(0, 1).reshape(3, 32, 16, 256).astype(F32)

    z_terms = scatter_group(z_near, z_far)
    output = (hidden + sum(t.astype(F32) for t in z_terms)).astype(BF16)
    return (
        output,
        grad_tokens,
        all_sum(dgain_attn),
        got[0],
        got[1],
        got[2],
        got[3].T,
        all_sum(dgain_moe),
        back[0],
        back[1],
        jnp.swapaxes(back[2], 1, 2),
    )


def solution(mesh):
    split = Mesh(mesh.devices.reshape(4, 2, 4, 2, 2), ("y", "xh", "z", "c", "xl"))
    dp = ("y", "xh", "z", "c")
    rows = P((*dp, "xl"), None)
    outs = (
        rows,
        rows,
        P(),
        P(dp, "xl"),
        P(dp, "xl"),
        P(dp, "xl"),
        P("xl", dp),
        P(),
        P(None, dp, "xl"),
        P(None, dp, "xl"),
        P(None, "xl", dp),
    )
    ins = (
        rows,
        P(),
        P(dp, "xl"),
        P(dp, "xl"),
        P(dp, "xl"),
        P("xl", dp),
        P(),
        P(None, dp, "xl"),
        P(None, dp, "xl"),
        P(None, "xl", dp),
        P(dp, None),
        P(dp, None),
        rows,
    )
    return jax.shard_map(on_device, mesh=split, in_specs=ins, out_specs=outs, check_vma=False)
```

time: 3510 us -> 487 us (0.14)
  waiting for transfers between devices: 3000 us -> 188 us
  matrix products: 201 us -> 0.81 us
  local copies, waits for them, and re-layouts: 154 us -> 16.1 us
  starting transfers between devices: 1.1 us -> 114 us
  Pallas kernels: 0 us -> 107 us
  blocking collectives: 67.5 us -> 17 us
    reduce_scatter x11 -> x0, waiting for transfers between devices: 2420 us -> none  [the longest x1 387 us: on_device(): lax.psum_scatter(gate_term, 'dp', scatter_dimension=1, tiled=True)]
    all_gather x11 -> x1, waiting for transfers between devices: 576 us -> 0.01 us  [on_device(): experts = lax.all_gather(owned, ('y', 'z'), axis=0)]
    dot_general x27 -> x1, matrix products: 201 us -> 0.81 us  [route_tables(): count = jnp.dot(named.astype(BF16), before, preferred_element_type=F32)]
    ppermute x0 -> x102, waiting for transfers between devices: none -> 179 us  [the longest x45 136 us: swap_x(): return lax.ppermute(value, ('xh', 'xl'), [(i, i ^ bits) for i in range(4)])]
    gather x4 -> x0, local copies, waits for them, and re-layouts: 114 us -> none  [the longest x1 29.5 us: on_device(): picked = expert_out[destination].reshape(length, route_count, -1)]
    ppermute x0 -> x102, starting transfers between devices: none -> 110 us  [the longest x45 65.1 us: swap_x(): return lax.ppermute(value, ('xh', 'xl'), [(i, i ^ bits) for i in range(4)])]
    pallas_call x0 -> x10, Pallas kernels: none -> 107 us  [the longest x9 56.8 us: kernel_call(): pl.pallas_call(body, out_shape=outs, in_specs=specs, out_specs=whole(len(...]
    psum x1 -> x0, blocking collectives: 67.5 us -> none  [on_device(): gain_sums = lax.psum((gain_attn_term, gain_moe_term), ('dp', 'tensor'))]
  transfers between devices with their start and end apart: 22 -> 105, of which waited for: 18 -> 32; matrix products, arithmetic and copies ran while one was open for 8% -> 7% of each run, Pallas kernels for 0% -> 12%
where the time goes in v1:
time: 487 us; the launch traced here: 479 us
  waiting for transfers between devices  188 us (39%)
  starting transfers between devices  114 us (23%)
  Pallas kernels  107 us (22%)
  other arithmetic  21 us (4%)
  blocking collectives  17 us (3%)
  local copies, waits for them, and re-layouts  16.1 us (3%)
  between operations  15.3 us (3%)
    ppermute x45, waiting for transfers between devices, swap_x(): return lax.ppermute(value, ('xh', 'xl'), [(i, i ^ bits) for i in range(4)])  136 us
    ppermute x45, starting transfers between devices, swap_x(): return lax.ppermute(value, ('xh', 'xl'), [(i, i ^ bits) for i in range(4)])  65.1 us
    pallas_call x9, Pallas kernels, kernel_call(): pl.pallas_call(body, out_shape=outs, in_specs=specs, out_specs=whole(len(...  56.8 us
    pallas_call x1, Pallas kernels, run_experts(): pl.pallas_call(expert_body, grid=(LOCAL_E,), out_shape=(blocks,) * 4 + (s...  49.7 us
    ppermute x24, starting transfers between devices, swap_4(): return lax.ppermute(value, axis, [(i, i ^ bits) for i in range(4)])  39.1 us
    ppermute x24, waiting for transfers between devices, swap_4(): return lax.ppermute(value, axis, [(i, i ^ bits) for i in range(4)])  38.3 us
    all_to_all x1, blocking collectives, on_device(): owned = lax.all_to_all(local, ('c', 'xh', 'xl'), 0, 0, tiled=True)  17 us
  transfers between devices with their start and end apart: 105, of which 32 were waited for; matrix products, arithmetic and copies ran while one was open for 7% of the time, Pallas kernels for 12%

profile of v1, /device:TPU:0, one launch (start us, length us, event | category | flops | bytes accessed | tf_op | source)
XLA Modules:
  0.0 478.8 jit_solution(16754565992052479398)
XLA Ops:
  8.5 17.0 %all_to_all.10 = bf16[8,3,4,16,256]{4,3,2,1,0:T(8,128)(2,1)} all-to-all(bf16[8,3,4,16,256]{4,3,2,1,0:T(8,128)(2,1)S(1)} %maximum_bitcast_fusion), channel_id=1, replica_groups=mesh['y'=4,'xh'=2,'z'=4,'c'=2,'xl'=2] {'c','xh','xl'}, dimensions={0} | all-to-all | bytes 1572864 | tf_op jit(solution)/shard_map/all_to_all | solution.py:406
  34.7 3.6 collective-permute-start.12
  46.7 3.0 collective-permute-start.15
  49.8 9.7 %collective-permute-done.14.p1 = bf16[4,64,512]{2,1,0:T(8,128)(2,1)S(1)} collective-permute-done((bf16[4,64,512]{2,1,0:T(8,128)(2,1)S(1)}, bf16[4,64,512]{2,1,0:T(8,128)(2,1)S(1)}, u32[]{:S(2)}, u32[]{:S(2)}) %collective-permute-start.14) | collective-permute-done | bytes 262176 | tf_op jit(solution)/shard_map/ppermute | solution.py:28
  59.5 6.8 %collective-permute-done.15.p2 = bf16[4,64,512]{2,1,0:T(8,128)(2,1)S(1)} collective-permute-done((bf16[4,64,512]{2,1,0:T(8,128)(2,1)S(1)}, bf16[4,64,512]{2,1,0:T(8,128)(2,1)S(1)}, u32[]{:S(2)}, u32[]{:S(2)}) %collective-permute-start.15) | collective-permute-done | bytes 262176 | tf_op jit(solution)/shard_map/ppermute | solution.py:28
  69.4 5.5 %collective-permute-done.16.p3 = bf16[4,64,512]{2,1,0:T(8,128)(2,1)} collective-permute-done((bf16[4,64,512]{2,1,0:T(8,128)(2,1)S(1)}, bf16[4,64,512]{2,1,0:T(8,128)(2,1)}, u32[]{:S(2)}, u32[]{:S(2)}) %collective-permute-start.16) | collective-permute-done | bytes 262176 | tf_op jit(solution)/shard_map/ppermute | solution.py:28
  85.1 10.8 %attend.1 = (bf16[4,512,1024]{2,1,0:T(8,128)(2,1)}, bf16[4,512,384]{2,1,0:T(8,128)(2,1)}, bf16[4,256,128]{2,1,0:T(8,128)(2,1)}, bf16[4,256,128]{2,1,0:T(8,128)(2,1)}) custom-call(bf16[256,1024]{1,0:T(8,128)(2,1)} %refs_12_.1, bf16[256,1024]{1,0:T(8,128)(2,1)} %collective-permute-done.refs_1_, bf16[256,1024]{1,0:T(8,128)(2,1)} %collective-permute-done.1.refs_2_, ...), custom_call_target="tpu_custom_call" | custom-call | tf_op jit(solution)/shard_map/attend/pallas_call | solution.py:65
  102.4 6.5 %collective-permute-done.36.refs_10_ = bf16[256,1024]{1,0:T(8,128)(2,1)S(1)} collective-permute-done((bf16[256,1024]{1,0:T(8,128)(2,1)S(1)}, bf16[256,1024]{1,0:T(8,128)(2,1)S(1)}, u32[]{:S(2)}, u32[]{:S(2)}) %collective-permute-start.36) | collective-permute-done | bytes 524320 | tf_op jit(solution)/shard_map/ppermute | solution.py:20
  111.7 5.6 %collective-permute-done.23.refs_9_ = bf16[1024,128]{1,0:T(8,128)(2,1)S(1)} collective-permute-done((bf16[1024,128]{1,0:T(8,128)(2,1)S(1)}, bf16[1024,128]{1,0:T(8,128)(2,1)S(1)}, u32[]{:S(2)}, u32[]{:S(2)}) %collective-permute-start.23) | collective-permute-done | bytes 262176 | tf_op jit(solution)/shard_map/ppermute | solution.py:20
  126.9 7.1 %collective-permute-done.20.refs_5_ = bf16[2,256,128]{2,1,0:T(8,128)(2,1)S(1)} collective-permute-done((bf16[2,256,128]{2,1,0:T(8,128)(2,1)}, bf16[2,256,128]{2,1,0:T(8,128)(2,1)S(1)}, u32[]{:S(2)}, u32[]{:S(2)}) %collective-permute-start.20) | collective-permute-done | bytes 131104 | tf_op jit(solution)/shard_map/ppermute | solution.py:20
  137.2 4.8 project.1
  148.8 8.4 %collective-permute-done.28.refs_1_ = bf16[256,1024]{1,0:T(8,128)(2,1)} collective-permute-done((bf16[256,1024]{1,0:T(8,128)(2,1)}, bf16[256,1024]{1,0:T(8,128)(2,1)}, u32[]{:S(2)}, u32[]{:S(2)}) %collective-permute-start.28) | collective-permute-done | bytes 524320 | tf_op jit(solution)/shard_map/ppermute | solution.py:20
  157.2 10.8 %collective-permute-done.29.refs_2_ = bf16[256,1024]{1,0:T(8,128)(2,1)} collective-permute-done((bf16[256,1024]{1,0:T(8,128)(2,1)}, bf16[256,1024]{1,0:T(8,128)(2,1)}, u32[]{:S(2)}, u32[]{:S(2)}) %collective-permute-start.29) | collective-permute-done | bytes 524320 | tf_op jit(solution)/shard_map/ppermute | solution.py:20
  173.8 49.7 %experts.1 = (bf16[4,256,1024]{2,1,0:T(8,128)(2,1)}, bf16[4,256,1024]{2,1,0:T(8,128)(2,1)}, bf16[4,256,1024]{2,1,0:T(8,128)(2,1)}, bf16[4,256,1024]{2,1,0:T(8,128)(2,1)}, bf16[16,8,3,4,16,256]{5,4,3,2,1,0:T(8,128)(2,1)}) custom-call(bf16[256,1024]{1,0:T(8,128)(2,1)} %get-tuple-element.42.refs_0_, bf16[256,1024]{1,0:T(8,128)(2,1)} %collective-permute-done.28.refs_1_, ...), custom_call_target="tpu_custom_call" | custom-call | tf_op jit(solution)/shard_map/experts/pallas_call | solution.py:219
  224.3 4.0 collective-permute-done.49
  233.6 12.8 %collective-permute-done.50.g1 = bf16[256,1024]{1,0:T(8,128)(2,1)S(1)} collective-permute-done((bf16[256,1024]{1,0:T(8,128)(2,1)S(1)}, bf16[256,1024]{1,0:T(8,128)(2,1)S(1)}, u32[]{:S(2)}, u32[]{:S(2)}) %collective-permute-start.50) | collective-permute-done | bytes 524320 | tf_op jit(solution)/shard_map/ppermute | solution.py:20
  246.4 10.4 %collective-permute-done.51.g2 = bf16[256,1024]{1,0:T(8,128)(2,1)S(1)} collective-permute-done((bf16[256,1024]{1,0:T(8,128)(2,1)S(1)}, bf16[256,1024]{1,0:T(8,128)(2,1)S(1)}, u32[]{:S(2)}, u32[]{:S(2)}) %collective-permute-start.51) | collective-permute-done | bytes 524320 | tf_op jit(solution)/shard_map/ppermute | solution.py:20
  257.8 5.1 %hidden_back.1 = (f32[256,1024]{1,0:T(8,128)}, bf16[256,1024]{1,0:T(8,128)(2,1)}, bf16[4,256,128]{2,1,0:T(8,128)(2,1)}, bf16[4,256,128]{2,1,0:T(8,128)(2,1)}, f32[1,1024]{1,0:T(1,128)}) custom-call(bf16[256,1024]{1,0:T(8,128)(2,1)} %get-tuple-element.66.g0, bf16[256,1024]{1,0:T(8,128)(2,1)} %copy-done.26, bf16[256,1024]{1,0:T(8,128)(2,1)} %copy-done.27, ...), custom_call_target="tpu_custom_call" | custom-call | tf_op jit(solution)/shard_map/hidden_back/pallas_call | solution.py:65
  274.9 3.2 collective-permute-start.94
  279.2 14.2 %attend_back.1 = (bf16[4,256,384]{2,1,0:T(8,128)(2,1)}, bf16[4,256,384]{2,1,0:T(8,128)(2,1)}) custom-call(bf16[4,512,384]{2,1,0:T(8,128)(2,1)} %get-tuple-element.45.qkv, bf16[2,256,128]{2,1,0:T(8,128)(2,1)} %pad_maximum_fusion.12.m0, bf16[2,256,128]{2,1,0:T(8,128)(2,1)} %copy-done.48, bf16[2,256,128]{2,1,0:T(8,128)(2,1)} %copy-done.47, ...), custom_call_target="tpu_custom_call" | custom-call | tf_op jit(solution)/shard_map/attend_back/pallas_call | solution.py:65
  293.3 7.5 %attend_grad.1 = (bf16[4,4,64,384]{3,2,1,0:T(8,128)(2,1)}, f32[1,1024]{1,0:T(1,128)}) custom-call(s32[2]{0:T(128)} %pad_add_fusion.ids, bf16[4,512,1024]{2,1,0:T(8,128)(2,1)} %get-tuple-element.54.n1, bf16[4,256,384]{2,1,0:T(8,128)(2,1)} %get-tuple-element.51.near, bf16[4,256,384]{2,1,0:T(8,128)(2,1)} %get-tuple-element.52.far, ...), custom_call_target="tpu_custom_call" | custom-call | tf_op jit(solution)/shard_map/attend_grad/pallas_call | solution.py:65
  306.4 4.3 collective-permute-start.70
  317.1 21.4 %collective-permute-done.71 = f32[8,128]{1,0:T(8,128)S(1)} collective-permute-done((f32[8,128]{1,0:T(8,128)S(1)}, f32[8,128]{1,0:T(8,128)S(1)}, u32[]{:S(2)}, u32[]{:S(2)}) %collective-permute-start.71) | collective-permute-done | bytes 4128 | tf_op jit(solution)/shard_map/ppermute | solution.py:20
  358.1 6.1 %collective-permute-done.80.w2 = bf16[1024,128]{1,0:T(8,128)(2,1)S(1)} collective-permute-done((bf16[1024,128]{1,0:T(8,128)(2,1)S(1)}, bf16[1024,128]{1,0:T(8,128)(2,1)S(1)}, u32[]{:S(2)}, u32[]{:S(2)}) %collective-permute-start.80) | collective-permute-done | bytes 262176 | tf_op jit(solution)/shard_map/ppermute | solution.py:20
  365.4 24.0 %collective-permute-done.81.w3 = bf16[1024,128]{1,0:T(8,128)(2,1)S(1)} collective-permute-done((bf16[1024,128]{1,0:T(8,128)(2,1)S(1)}, bf16[1024,128]{1,0:T(8,128)(2,1)S(1)}, u32[]{:S(2)}, u32[]{:S(2)}) %collective-permute-start.81) | collective-permute-done | bytes 262176 | tf_op jit(solution)/shard_map/ppermute | solution.py:20
  399.5 3.0 collective-permute-done.82
  402.5 3.8 collective-permute-done.83
  419.4 3.1 collective-permute-start.76
  429.4 12.6 %collective-permute-done.60.refs_3_ = bf16[2,256,384]{2,1,0:T(8,128)(2,1)S(1)} collective-permute-done((bf16[2,256,384]{2,1,0:T(8,128)(2,1)S(1)}, bf16[2,256,384]{2,1,0:T(8,128)(2,1)S(1)}, u32[]{:S(2)}, u32[]{:S(2)}) %collective-permute-start.60) | collective-permute-done | bytes 393248 | tf_op jit(solution)/shard_map/ppermute | solution.py:20
  447.2 7.0 %tokens_back.1 = bf16[256,1024]{1,0:T(8,128)(2,1)} custom-call(bf16[2,256,384]{2,1,0:T(8,128)(2,1)} %pad_maximum_fusion.refs_0_, bf16[2,256,384]{2,1,0:T(8,128)(2,1)} %copy-done.31, bf16[2,256,384]{2,1,0:T(8,128)(2,1)} %copy-done.30, bf16[2,256,384]{2,1,0:T(8,128)(2,1)} %copy-done.29, bf16[1024,384]{1,0:T(8,128)(2,1)} %get-tuple-element.37.refs_9_.refs_4_.w_qkv, ...), custom_call_target="tpu_custom_call" | custom-call | tf_op jit(solution)/shard_map/tokens_back/pallas_call | solution.py:65
  454.4 3.6 all-to-all-start.1
  460.7 9.6 %all-to-all-done.1 = bf16[8,3,4,16,256]{4,3,2,1,0:T(8,128)(2,1)S(1)} async-done(((bf16[8,3,4,16,256]{4,3,2,1,0:T(8,128)(2,1)}), bf16[8,3,4,16,256]{4,3,2,1,0:T(8,128)(2,1)S(1)}, u32[]{:S(2)}, u32[]{:S(2)}) %all-to-all-start.1) | async-done | bytes 786464 | tf_op jit(solution)/shard_map/all_to_all | solution.py:496
  (408 shorter events, 158.5 us)
Async XLA Ops:
  7.2 165.7 %all-gather.3.cloned.1.call-start = ((), (), s32[]{:S(2)}) async-start(), calls=%async_computation.3 | async-start | bytes 13369344 | tf_op jit(solution)/shard_map/all_gather | solution.py:407
  25.5 428.9 %reduce-scatter.4.cloned.1.call-start = ((), (), s32[]{:S(2)}) async-start(), calls=%async_computation.4 | async-start | bytes 13369344
  29.9 37.2 %collective-permute-start = (bf16[256,1024]{1,0:T(8,128)(2,1)S(1)}, bf16[256,1024]{1,0:T(8,128)(2,1)}, u32[]{:S(2)}, u32[]{:S(2)}) collective-permute-start(bf16[256,1024]{1,0:T(8,128)(2,1)S(1)} %copy-done.1), channel_id=1, source_target_pairs={{0,1},{1,0},{16,17},{17,16},{2,3},{3,2},{18,19},{19,18},{4,5},{5,4... | collective-permute-start | bytes 1572872 | tf_op jit(solution)/shard_map/ppermute | solution.py:20
  38.3 29.8 %collective-permute-start.1 = (bf16[256,1024]{1,0:T(8,128)(2,1)S(1)}, bf16[256,1024]{1,0:T(8,128)(2,1)}, u32[]{:S(2)}, u32[]{:S(2)}) collective-permute-start(bf16[256,1024]{1,0:T(8,128)(2,1)S(1)} %copy-done.1), channel_id=1, source_target_pairs={{0,16},{1,17},{16,0},{17,1},{2,18},{3,19},{18,2},{19,3},{4,20},{5,... | collective-permute-start | bytes 1572872 | tf_op jit(solution)/shard_map/ppermute | solution.py:20
  40.9 27.7 %collective-permute-start.2 = (bf16[256,1024]{1,0:T(8,128)(2,1)S(1)}, bf16[256,1024]{1,0:T(8,128)(2,1)}, u32[]{:S(2)}, u32[]{:S(2)}) collective-permute-start(bf16[256,1024]{1,0:T(8,128)(2,1)S(1)} %copy-done.1), channel_id=1, source_target_pairs={{0,17},{1,16},{16,1},{17,0},{2,19},{3,18},{18,3},{19,2},{4,21},{5,... | collective-permute-start | bytes 1572872 | tf_op jit(solution)/shard_map/ppermute | solution.py:20
  74.9 25.4 %collective-permute-start.35 = (bf16[256,1024]{1,0:T(8,128)(2,1)S(1)}, bf16[256,1024]{1,0:T(8,128)(2,1)S(1)}, u32[]{:S(2)}, u32[]{:S(2)}) collective-permute-start(bf16[256,1024]{1,0:T(8,128)(2,1)S(1)} %copy-done.7), channel_id=1, source_target_pairs={{0,1},{1,0},{16,17},{17,16},{2,3},{3,2},{18,19},{19,18},{4,5},{5,4... | collective-permute-start | bytes 1572872 | tf_op jit(solution)/shard_map/ppermute | solution.py:20
  79.8 21.0 %collective-permute-start.21 = (bf16[1024,128]{1,0:T(8,128)(2,1)}, bf16[1024,128]{1,0:T(8,128)(2,1)S(1)}, u32[]{:S(2)}, u32[]{:S(2)}) collective-permute-start(bf16[1024,128]{1,0:T(8,128)(2,1)} %get-tuple-element.40.refs_6_), channel_id=1, source_target_pairs={{0,1},{1,0},{16,17},{17,16},{2,3},{3,2},{18,19},{19,18},{4,5},{5,4... | collective-permute-start | bytes 786440 | tf_op jit(solution)/shard_map/ppermute | solution.py:20
  83.2 25.7 %collective-permute-start.36 = (bf16[256,1024]{1,0:T(8,128)(2,1)S(1)}, bf16[256,1024]{1,0:T(8,128)(2,1)S(1)}, u32[]{:S(2)}, u32[]{:S(2)}) collective-permute-start(bf16[256,1024]{1,0:T(8,128)(2,1)S(1)} %copy-done.7), channel_id=1, source_target_pairs={{0,16},{1,17},{16,0},{17,1},{2,18},{3,19},{18,2},{19,3},{4,20},{5,... | collective-permute-start | bytes 1572872 | tf_op jit(solution)/shard_map/ppermute | solution.py:20
  108.9 33.5 %collective-permute-start.37 = (bf16[256,1024]{1,0:T(8,128)(2,1)S(1)}, bf16[256,1024]{1,0:T(8,128)(2,1)S(1)}, u32[]{:S(2)}, u32[]{:S(2)}) collective-permute-start(bf16[256,1024]{1,0:T(8,128)(2,1)S(1)} %copy-done.7), channel_id=1, source_target_pairs={{0,17},{1,16},{16,1},{17,0},{2,19},{3,18},{18,3},{19,2},{4,21},{5,... | collective-permute-start | bytes 1572872 | tf_op jit(solution)/shard_map/ppermute | solution.py:20
  111.7 32.8 %collective-permute-start.38 = (bf16[256,1024]{1,0:T(8,128)(2,1)S(1)}, bf16[256,1024]{1,0:T(8,128)(2,1)S(1)}, u32[]{:S(2)}, u32[]{:S(2)}) collective-permute-start(bf16[256,1024]{1,0:T(8,128)(2,1)S(1)} %copy-done.7), channel_id=1, source_target_pairs={{0,2},{2,0},{1,3},{3,1},{4,6},{6,4},{5,7},{7,5},{8,10},{10,8},{9,1... | collective-permute-start | bytes 1572872 | tf_op jit(solution)/shard_map/ppermute | solution.py:24
  142.4 25.7 %collective-permute-start.29 = (bf16[256,1024]{1,0:T(8,128)(2,1)}, bf16[256,1024]{1,0:T(8,128)(2,1)}, u32[]{:S(2)}, u32[]{:S(2)}) collective-permute-start(bf16[256,1024]{1,0:T(8,128)(2,1)} %get-tuple-element.42.refs_0_), channel_id=1, source_target_pairs={{0,16},{1,17},{16,0},{17,1},{2,18},{3,19},{18,2},{19,3},{4,20},{5,... | collective-permute-start | bytes 1572872 | tf_op jit(solution)/shard_map/ppermute | solution.py:20
  144.5 26.0 %collective-permute-start.30 = (bf16[256,1024]{1,0:T(8,128)(2,1)}, bf16[256,1024]{1,0:T(8,128)(2,1)S(1)}, u32[]{:S(2)}, u32[]{:S(2)}) collective-permute-start(bf16[256,1024]{1,0:T(8,128)(2,1)} %get-tuple-element.42.refs_0_), channel_id=1, source_target_pairs={{0,17},{1,16},{16,1},{17,0},{2,19},{3,18},{18,3},{19,2},{4,21},{5,... | collective-permute-start | bytes 1572872 | tf_op jit(solution)/shard_map/ppermute | solution.py:20
  148.2 24.5 %collective-permute-start.41 = (bf16[256,1024]{1,0:T(8,128)(2,1)S(1)}, bf16[256,1024]{1,0:T(8,128)(2,1)S(1)}, u32[]{:S(2)}, u32[]{:S(2)}) collective-permute-start(bf16[256,1024]{1,0:T(8,128)(2,1)S(1)} %collective-permute-done.37.refs_11_), channel_id=1, source_target_pairs={{0,2},{2,0},{1,3},{3,1},{4,6},{6,4},{5,7},{7,5},{8,10},{10,8},{9,1... | collective-permute-start | bytes 1572872 | tf_op jit(solution)/shard_map/ppermute | solution.py:24
  148.3 24.4 %collective-permute-start.31 = (bf16[256,1024]{1,0:T(8,128)(2,1)}, bf16[256,1024]{1,0:T(8,128)(2,1)S(1)}, u32[]{:S(2)}, u32[]{:S(2)}) collective-permute-start(bf16[256,1024]{1,0:T(8,128)(2,1)} %get-tuple-element.42.refs_0_), channel_id=1, source_target_pairs={{0,2},{2,0},{1,3},{3,1},{4,6},{6,4},{5,7},{7,5},{8,10},{10,8},{9,1... | collective-permute-start | bytes 1572872 | tf_op jit(solution)/shard_map/ppermute | solution.py:24
  224.1 82.3 %collective-permute-start.45 = (bf16[4,256,1024]{2,1,0:T(8,128)(2,1)}, bf16[4,256,1024]{2,1,0:T(8,128)(2,1)}, u32[]{:S(2)}, u32[]{:S(2)}) collective-permute-start(bf16[4,256,1024]{2,1,0:T(8,128)(2,1)} %get-tuple-element.44), channel_id=1, source_target_pairs={{0,2},{2,0},{1,3},{3,1},{4,6},{6,4},{5,7},{7,5},{8,10},{10,8},{9,1... | collective-permute-start | bytes 6291464 | tf_op jit(solution)/shard_map/ppermute | solution.py:24
  230.4 26.4 %collective-permute-start.51 = (bf16[256,1024]{1,0:T(8,128)(2,1)S(1)}, bf16[256,1024]{1,0:T(8,128)(2,1)S(1)}, u32[]{:S(2)}, u32[]{:S(2)}) collective-permute-start(bf16[256,1024]{1,0:T(8,128)(2,1)S(1)} %get-tuple-element.64), channel_id=1, source_target_pairs={{0,17},{1,16},{16,1},{17,0},{2,19},{3,18},{18,3},{19,2},{4,21},{5,... | collective-permute-start | bytes 1572872 | tf_op jit(solution)/shard_map/ppermute | solution.py:20
  232.4 24.4 %collective-permute-start.52 = (bf16[256,1024]{1,0:T(8,128)(2,1)S(1)}, bf16[256,1024]{1,0:T(8,128)(2,1)S(1)}, u32[]{:S(2)}, u32[]{:S(2)}) collective-permute-start(bf16[256,1024]{1,0:T(8,128)(2,1)S(1)} %get-tuple-element.63), channel_id=1, source_target_pairs={{0,1},{1,0},{16,17},{17,16},{2,3},{3,2},{18,19},{19,18},{4,5},{5,4... | collective-permute-start | bytes 1572872 | tf_op jit(solution)/shard_map/ppermute | solution.py:20
  272.1 67.8 %collective-permute-start.78 = (bf16[4,1024,128]{2,1,0:T(8,128)(2,1)}, bf16[4,1024,128]{2,1,0:T(8,128)(2,1)S(1)}, u32[]{:S(2)}, u32[]{:S(2)}) collective-permute-start(bf16[4,1024,128]{2,1,0:T(8,128)(2,1)} %get-tuple-element.60), channel_id=1, source_target_pairs={{0,2},{2,0},{1,3},{3,1},{4,6},{6,4},{5,7},{7,5},{8,10},{10,8},{9,1... | collective-permute-start | bytes 3145736 | tf_op jit(solution)/shard_map/ppermute | solution.py:24
  273.8 27.1 %collective-permute-start.93 = (f32[8,128]{1,0:T(8,128)S(1)}, f32[8,128]{1,0:T(8,128)S(1)}, u32[]{:S(2)}, u32[]{:S(2)}) collective-permute-start(f32[8,128]{1,0:T(8,128)S(1)} %add.217), channel_id=1, source_target_pairs={{0,1},{1,0},{16,17},{17,16},{2,3},{3,2},{18,19},{19,18},{4,5},{5,4... | collective-permute-start | bytes 12296 | tf_op jit(solution)/shard_map/ppermute | solution.py:20
  274.9 26.0 %collective-permute-start.94 = (f32[8,128]{1,0:T(8,128)S(1)}, f32[8,128]{1,0:T(8,128)S(1)}, u32[]{:S(2)}, u32[]{:S(2)}) collective-permute-start(f32[8,128]{1,0:T(8,128)S(1)} %add.217), channel_id=1, source_target_pairs={{0,16},{1,17},{16,0},{17,1},{2,18},{3,19},{18,2},{19,3},{4,20},{5,... | collective-permute-start | bytes 12296 | tf_op jit(solution)/shard_map/ppermute | solution.py:20
  278.1 22.8 %collective-permute-start.95 = (f32[8,128]{1,0:T(8,128)S(1)}, f32[8,128]{1,0:T(8,128)S(1)}, u32[]{:S(2)}, u32[]{:S(2)}) collective-permute-start(f32[8,128]{1,0:T(8,128)S(1)} %add.217), channel_id=1, source_target_pairs={{0,17},{1,16},{16,1},{17,0},{2,19},{3,18},{18,3},{19,2},{4,21},{5,... | collective-permute-start | bytes 12296 | tf_op jit(solution)/shard_map/ppermute | solution.py:20
  312.9 28.4 %collective-permute-start.46 = (bf16[256,1024]{1,0:T(8,128)(2,1)S(1)}, bf16[256,1024]{1,0:T(8,128)(2,1)S(1)}, u32[]{:S(2)}, u32[]{:S(2)}) collective-permute-start(bf16[256,1024]{1,0:T(8,128)(2,1)S(1)} %get-tuple-element.67), channel_id=1, source_target_pairs={{0,16},{1,17},{16,0},{17,1},{2,18},{3,19},{18,2},{19,3},{4,20},{5,... | collective-permute-start | bytes 1572872 | tf_op jit(solution)/shard_map/ppermute | solution.py:20
  313.0 30.1 %collective-permute-start.47 = (bf16[256,1024]{1,0:T(8,128)(2,1)S(1)}, bf16[256,1024]{1,0:T(8,128)(2,1)S(1)}, u32[]{:S(2)}, u32[]{:S(2)}) collective-permute-start(bf16[256,1024]{1,0:T(8,128)(2,1)S(1)} %get-tuple-element.69), channel_id=1, source_target_pairs={{0,17},{1,16},{16,1},{17,0},{2,19},{3,18},{18,3},{19,2},{4,21},{5,... | collective-permute-start | bytes 1572872 | tf_op jit(solution)/shard_map/ppermute | solution.py:20
  315.1 27.9 %collective-permute-start.48 = (bf16[256,1024]{1,0:T(8,128)(2,1)S(1)}, bf16[256,1024]{1,0:T(8,128)(2,1)S(1)}, u32[]{:S(2)}, u32[]{:S(2)}) collective-permute-start(bf16[256,1024]{1,0:T(8,128)(2,1)S(1)} %get-tuple-element.68), channel_id=1, source_target_pairs={{0,1},{1,0},{16,17},{17,16},{2,3},{3,2},{18,19},{19,18},{4,5},{5,4... | collective-permute-start | bytes 1572872 | tf_op jit(solution)/shard_map/ppermute | solution.py:20
  316.4 22.1 %collective-permute-start.71 = (f32[8,128]{1,0:T(8,128)S(1)}, f32[8,128]{1,0:T(8,128)S(1)}, u32[]{:S(2)}, u32[]{:S(2)}) collective-permute-start(f32[8,128]{1,0:T(8,128)S(1)} %add.197), channel_id=1, source_target_pairs={{0,17},{1,16},{16,1},{17,0},{2,19},{3,18},{18,3},{19,2},{4,21},{5,... | collective-permute-start | bytes 12296 | tf_op jit(solution)/shard_map/ppermute | solution.py:20
  346.2 48.8 %collective-permute-start.61 = (bf16[1024,384]{1,0:T(8,128)(2,1)S(1)}, bf16[1024,384]{1,0:T(8,128)(2,1)S(1)}, u32[]{:S(2)}, u32[]{:S(2)}) collective-permute-start(bf16[1024,384]{1,0:T(8,128)(2,1)S(1)} %copy-done), channel_id=1, source_target_pairs={{0,1},{1,0},{16,17},{17,16},{2,3},{3,2},{18,19},{19,18},{4,5},{5,4... | collective-permute-start | bytes 2359304 | tf_op jit(solution)/shard_map/ppermute | solution.py:20
  347.1 48.7 %collective-permute-start.57 = (bf16[4,256,384]{2,1,0:T(8,128)(2,1)S(1)}, bf16[4,256,384]{2,1,0:T(8,128)(2,1)}, u32[]{:S(2)}, u32[]{:S(2)}) collective-permute-start(bf16[4,256,384]{2,1,0:T(8,128)(2,1)S(1)} %copy-done.12), channel_id=1, source_target_pairs={{0,2},{2,0},{1,3},{3,1},{4,6},{6,4},{5,7},{7,5},{8,10},{10,8},{9,1... | collective-permute-start | bytes 2359304 | tf_op jit(solution)/shard_map/ppermute | solution.py:24
  352.5 46.9 %collective-permute-start.62 = (bf16[1024,384]{1,0:T(8,128)(2,1)S(1)}, bf16[1024,384]{1,0:T(8,128)(2,1)}, u32[]{:S(2)}, u32[]{:S(2)}) collective-permute-start(bf16[1024,384]{1,0:T(8,128)(2,1)S(1)} %copy-done), channel_id=1, source_target_pairs={{0,16},{1,17},{16,0},{17,1},{2,18},{3,19},{18,2},{19,3},{4,20},{5,... | collective-permute-start | bytes 2359304 | tf_op jit(solution)/shard_map/ppermute | solution.py:20
  356.6 32.7 %collective-permute-start.81 = (bf16[1024,128]{1,0:T(8,128)(2,1)S(1)}, bf16[1024,128]{1,0:T(8,128)(2,1)S(1)}, u32[]{:S(2)}, u32[]{:S(2)}) collective-permute-start(bf16[1024,128]{1,0:T(8,128)(2,1)S(1)} %get-tuple-element.70), channel_id=1, source_target_pairs={{0,1},{1,0},{16,17},{17,16},{2,3},{3,2},{18,19},{19,18},{4,5},{5,4... | collective-permute-start | bytes 786440 | tf_op jit(solution)/shard_map/ppermute | solution.py:20
  364.2 46.6 %collective-permute-start.63 = (bf16[1024,384]{1,0:T(8,128)(2,1)S(1)}, bf16[1024,384]{1,0:T(8,128)(2,1)}, u32[]{:S(2)}, u32[]{:S(2)}) collective-permute-start(bf16[1024,384]{1,0:T(8,128)(2,1)S(1)} %copy-done), channel_id=1, source_target_pairs={{0,17},{1,16},{16,1},{17,0},{2,19},{3,18},{18,3},{19,2},{4,21},{5,... | collective-permute-start | bytes 2359304 | tf_op jit(solution)/shard_map/ppermute | solution.py:20
  425.7 20.6 %collective-permute-start.59 = (bf16[2,256,384]{2,1,0:T(8,128)(2,1)S(1)}, bf16[2,256,384]{2,1,0:T(8,128)(2,1)S(1)}, u32[]{:S(2)}, u32[]{:S(2)}) collective-permute-start(bf16[2,256,384]{2,1,0:T(8,128)(2,1)S(1)} %pad_maximum_fusion.2), channel_id=1, source_target_pairs={{0,16},{1,17},{16,0},{17,1},{2,18},{3,19},{18,2},{19,3},{4,20},{5,... | collective-permute-start | bytes 1179656 | tf_op jit(solution)/shard_map/ppermute | solution.py:20
  428.9 25.3 %collective-permute-start.88 = (f32[16,512]{1,0:T(8,128)S(1)}, f32[16,512]{1,0:T(8,128)S(1)}, u32[]{:S(2)}, u32[]{:S(2)}) collective-permute-start(f32[16,512]{1,0:T(8,128)S(1)} %get-tuple-element.114), channel_id=1, source_target_pairs={{0,2},{2,0},{1,3},{3,1},{4,6},{6,4},{5,7},{7,5},{8,10},{10,8},{9,1... | collective-permute-start | bytes 98312 | tf_op jit(solution)/shard_map/ppermute | solution.py:24
  (135 other events, 1754.3 us)
Sparse Core Ops, SparseCore 0:
  25.6 100.4 all-gather.2
  223.6 91.7 reduce-scatter.3
